TPU v7x, 256 devices: a whole 4x4x8 slice. The times are simulated.
256 devices in a mesh: dp: 4 (over x_hi, core), mp: 64 (over x_lo, y, z).
Axes of the slice: x: 4 (x_hi: 2, x_lo: 2; x = x_hi * 2 + x_lo), y: 4, z: 8, core: 2. Of those that a mesh axis runs over, the one named last changes fastest.
Arguments:
- tokens: bfloat16 [2304, 4096], P(('dp', 'mp')), may hold values from -6 to 6
- out_grad: bfloat16 [2304, 4096], P(('dp', 'mp')), may hold values from -6 to 6
- gate_weight: bfloat16 [16384, 4096], P('mp', 'dp'), may hold values from -0.125 to 0.125
- up_weight: bfloat16 [16384, 4096], P('mp', 'dp'), may hold values from -0.125 to 0.125
- down_weight: bfloat16 [16384, 4096], P('mp', 'dp'), may hold values from -0.0625 to 0.0625
- block_mask: int32 [3, 128, 32], replicated, may hold values 0 or 1
- assignment: int32 [128], P('mp'), may hold values from 0 to 127, each once
Outputs:
- input_grad: bfloat16 [2304, 4096], P(('dp', 'mp'))
- gate_grad_out: bfloat16 [16384, 4096], P('mp', 'dp')
- up_grad_out: bfloat16 [16384, 4096], P('mp', 'dp')
- down_grad_out: bfloat16 [16384, 4096], P('mp', 'dp')
Inputs may be any that keep to these rules, and one draw needn't show every extreme that they name: `assignment`: each of the 128 panel numbers appears once.
All inputs are finite; a program needn't handle non-finite values.
Results may differ from a plain program's by a relative error of at most 0.0049.
Values may be sent and summed in bfloat16 or wider, within the bound.
No kernel may reach another device: no remote copies, remote signals or barrier semaphores. Data moves between devices by JAX's collectives and lax.ppermute only.
A program may use at most 128 MiB of HBM per device.

v0:
```python
import jax
import jax.numpy as jnp
from jax import lax
from jax.sharding import PartitionSpec as P

BLK = 128


def spread_mask(rows):
    wide = jnp.repeat(jnp.repeat(rows, BLK, axis=0), BLK, axis=1)
    return wide.astype(jnp.bfloat16)


def outer_sum(left, right):
    return jnp.einsum("th,td->hd", left, right, preferred_element_type=jnp.float32)


def per_device(tokens, out_grad, gate_weight, up_weight, down_weight, block_mask, assignment):
    part_cols = gate_weight.shape[1]
    col_blocks = part_cols // BLK
    first_block = lax.axis_index("dp") * col_blocks
    panel_ids = lax.broadcasted_iota(jnp.int32, (assignment.shape[0], block_mask.shape[1]), 1)
    selector = (assignment[:, None] == panel_ids).astype(jnp.float32)
    slot_mask = jnp.einsum("sp,mpb->msb", selector, block_mask.astype(jnp.float32))
    local_mask = lax.dynamic_slice_in_dim(slot_mask, first_block, col_blocks, 2)
    gate_keep = spread_mask(local_mask[0])
    up_keep = spread_mask(local_mask[1])
    down_keep = spread_mask(local_mask[2])
    gate_full, up_full, down_full = (
        lax.all_gather(gate_weight * gate_keep, "dp", axis=1, tiled=True),
        lax.all_gather(up_weight * up_keep, "dp", axis=1, tiled=True),
        lax.all_gather(down_weight * down_keep, "dp", axis=1, tiled=True),
    )
    inputs, grads_out = (
        lax.all_gather(tokens, "mp", axis=0, tiled=True),
        lax.all_gather(out_grad, "mp", axis=0, tiled=True),
    )
    gate_pre = jnp.einsum("td,hd->th", inputs, gate_full, preferred_element_type=jnp.float32)
    up_pre = jnp.einsum("td,hd->th", inputs, up_full, preferred_element_type=jnp.float32)
    sigma = jax.nn.sigmoid(gate_pre)
    swish = gate_pre * sigma
    hidden = (swish * up_pre).astype(jnp.bfloat16)
    hidden_grad = jnp.einsum("td,hd->th", grads_out, down_full, preferred_element_type=jnp.float32)
    up_grad = (hidden_grad * swish).astype(jnp.bfloat16)
    gate_grad = (hidden_grad * up_pre * sigma * (1.0 + gate_pre * (1.0 - sigma))).astype(
        jnp.bfloat16
    )
    total = jnp.dot(gate_grad, gate_full, preferred_element_type=jnp.float32)
    input_grad = lax.psum_scatter(
        total + jnp.dot(up_grad, up_full, preferred_element_type=jnp.float32),
        "mp",
        scatter_dimension=0,
        tiled=True,
    ).astype(jnp.bfloat16)
    gate_part, up_part, down_part = (
        lax.psum_scatter(outer_sum(gate_grad, inputs), "dp", scatter_dimension=1, tiled=True),
        lax.psum_scatter(outer_sum(up_grad, inputs), "dp", scatter_dimension=1, tiled=True),
        lax.psum_scatter(outer_sum(hidden, grads_out), "dp", scatter_dimension=1, tiled=True),
    )
    gate_out = (gate_part * gate_keep).astype(jnp.bfloat16)
    up_out = (up_part * up_keep).astype(jnp.bfloat16)
    down_out = (down_part * down_keep).astype(jnp.bfloat16)
    return (input_grad, gate_out, up_out, down_out)


def solution(mesh):
    placed = (
        P(("dp", "mp"), None),
        P(("dp", "mp"), None),
        P("mp", "dp"),
        P("mp", "dp"),
        P("mp", "dp"),
        P(),
        P("mp"),
    )
    return jax.shard_map(
        per_device,
        mesh=mesh,
        in_specs=placed,
        out_specs=(P(("dp", "mp"), None), P("mp", "dp"), P("mp", "dp"), P("mp", "dp")),
        check_vma=False,
    )
```

profile of v0, /device:TPU:2, one launch (start us, length us, event | category | flops | bytes accessed | tf_op | source)
XLA Modules:
  0.0 1140.5 jit_solution(12114293916159827040)
XLA Ops:
  7.2 0.0 all-gather.16.cloned.1.call-start
  7.2 0.7 all-gather.16.cloned.1.call-update
  7.9 0.0 all-gather.14.cloned.1.call-start
  8.0 0.7 all-gather.14.cloned.1.call-update
  8.7 0.0 all-gather.12.cloned.1.call-start
  8.7 1.0 fusion.3
  9.7 0.1 fusion.7
  9.8 0.3 broadcast_in_dim.24
  10.2 1.9 bitcast_multiply_fusion
  12.1 0.0 all-gather.12.cloned.1.call-update
  12.1 0.0 all-gather.10.cloned.1.call-start
  12.2 0.3 broadcast_in_dim.22
  12.5 1.9 bitcast_multiply_fusion.1
  14.4 0.0 all-gather.10.cloned.1.call-update
  14.4 0.0 all-gather.8.cloned.1.call-start
  14.5 0.3 broadcast_in_dim.20
  14.8 0.9 bitcast_multiply_fusion.2
  15.7 0.0 all-gather.8.cloned.1.call-update
  15.7 0.0 reduce-scatter.8.cloned.1.call-start
  15.8 308.0 %all-gather.16.cloned.1.call-done = bf16[64,9,4096]{2,1,0:T(8,128)(2,1)} async-done(((bf16[1,9,4096]{2,1,0:T(8,128)(2,1)}), bf16[64,9,4096]{2,1,0:T(8,128)(2,1)}) %all-gather.16.cloned.1.call-update) | async-done | bytes 4718608 | tf_op jit(solution)/shard_map/all_gather | solution.py:35
  323.8 8.6 reshape.27
  332.3 302.5 %all-gather.14.cloned.1.call-done = bf16[64,9,4096]{2,1,0:T(8,128)(2,1)} async-done(((bf16[1,9,4096]{2,1,0:T(8,128)(2,1)}), bf16[64,9,4096]{2,1,0:T(8,128)(2,1)}) %all-gather.14.cloned.1.call-update) | async-done | bytes 4718608 | tf_op jit(solution)/shard_map/all_gather | solution.py:36
  634.9 8.5 reshape.25
  643.3 20.5 %all-gather.12.cloned.1.call-done = bf16[256,4096]{1,0:T(8,128)(2,1)} async-done(((bf16[256,1024]{1,0:T(8,128)(2,1)}), bf16[256,4096]{1,0:T(8,128)(2,1)}) %all-gather.12.cloned.1.call-update) | async-done | bytes 2097168 | tf_op jit(solution)/shard_map/all_gather | solution.py:30
  663.9 4.4 convolution_bitcast_fusion
  668.3 26.5 %all-gather.10.cloned.1.call-done = bf16[256,4096]{1,0:T(8,128)(2,1)} async-done(((bf16[256,1024]{1,0:T(8,128)(2,1)}), bf16[256,4096]{1,0:T(8,128)(2,1)}) %all-gather.10.cloned.1.call-update) | async-done | bytes 2097168 | tf_op jit(solution)/shard_map/all_gather | solution.py:31
  694.8 4.5 convolution_bitcast_fusion.1
  699.4 3.9 fusion.1
  703.2 0.0 reduce-scatter.8.cloned.1.call-update
  703.3 0.0 reduce-scatter.4.cloned.1.call-start
  703.3 22.4 %all-gather.8.cloned.1.call-done = bf16[256,4096]{1,0:T(8,128)(2,1)} async-done(((bf16[256,1024]{1,0:T(8,128)(2,1)}), bf16[256,4096]{1,0:T(8,128)(2,1)}) %all-gather.8.cloned.1.call-update) | async-done | bytes 2097168 | tf_op jit(solution)/shard_map/all_gather | solution.py:32
  725.7 4.5 multiply_convert_fusion.4
  730.2 0.0 copy-start.3
  730.2 6.2 fusion.12
  736.5 0.0 reduce-scatter.4.cloned.1.call-update
  736.5 0.2 reduce-scatter.6.cloned.1.call-start
  736.7 0.6 dynamic-slice.4
  738.0 0.0 slice-start
  738.0 3.3 fusion.11
  741.3 0.0 slice-start.1
  741.4 5.2 convolution_add_fusion
  746.5 3.8 fusion.13
  750.3 0.0 reduce-scatter.6.cloned.1.call-update
  750.4 375.1 %all-reduce.2 = bf16[576,4096]{1,0:T(8,128)(2,1)} all-reduce(f32[576,4096]{1,0:T(8,128)} %convolution_add_fusion), channel_id=2, replica_groups=mesh['dp'=4,'mp'=64] {'mp'}, use_global_device_ids=true, to_apply=%region_0.0.clone | all-reduce | flops 2359296 | bytes 14155776
  1125.5 1.6 dynamic-slice_convert_fusion
  1127.1 2.2 multiply_convert_fusion
  1129.3 2.2 multiply_convert_fusion.2
  1131.5 2.2 multiply_convert_fusion.1
  (17 shorter events, 0.1 us)
Async XLA Ops:
  7.2 7.7 copy-start.2
  7.2 316.6 %all-gather.16.cloned.1.call-start = ((), (), s32[]{:S(2)}) async-start(), calls=%async_computation.10 | async-start | bytes 8519680 | tf_op jit(solution)/shard_map/all_gather | solution.py:35
  7.9 627.0 %all-gather.14.cloned.1.call-start = ((), (), s32[]{:S(2)}) async-start(), calls=%async_computation.9 | async-start | bytes 8519680 | tf_op jit(solution)/shard_map/all_gather | solution.py:36
  8.7 655.2 %all-gather.12.cloned.1.call-start = ((), (), s32[]{:S(2)}) async-start(), calls=%async_computation.5 | async-start | bytes 2621440 | tf_op jit(solution)/shard_map/all_gather | solution.py:30
  12.1 682.7 %all-gather.10.cloned.1.call-start = ((), (), s32[]{:S(2)}) async-start(), calls=%async_computation.4 | async-start | bytes 2621440 | tf_op jit(solution)/shard_map/all_gather | solution.py:31
  14.4 711.3 %all-gather.8.cloned.1.call-start = ((), (), s32[]{:S(2)}) async-start(), calls=%async_computation.3 | async-start | bytes 2621440 | tf_op jit(solution)/shard_map/all_gather | solution.py:32
  15.7 1111.4 %reduce-scatter.8.cloned.1.call-start = ((), (), s32[]{:S(2)}) async-start(), calls=%async_computation.8 | async-start | bytes 5242880 | tf_op jit(solution)/shard_map/reduce_scatter | solution.py:58
  694.8 4.5 copy-start
  703.3 426.0 %reduce-scatter.4.cloned.1.call-start = ((), (), s32[]{:S(2)}) async-start(), calls=%async_computation.6 | async-start | bytes 5242880 | tf_op jit(solution)/shard_map/reduce_scatter | solution.py:56
  730.2 6.5 copy-start.3
  736.5 395.0 %reduce-scatter.6.cloned.1.call-start = ((), (), s32[]{:S(2)}) async-start(), calls=%async_computation.7 | async-start | bytes 5242880 | tf_op jit(solution)/shard_map/reduce_scatter | solution.py:57
  738.0 3.4 copy-start.1
  738.0 8.5 slice-start
  741.3 5.2 slice-start.1
Sparse Core Ops, SparseCore 0:
  9.8 313.9 all-gather.15
  325.5 309.2 all-gather.13
  637.3 26.5 all-gather.11
  666.1 28.6 all-gather.9
  697.0 28.6 all-gather.7
  728.4 56.0 reduce-scatter.7
  787.4 85.8 reduce-scatter.3
  876.1 83.7 reduce-scatter.5
where the time goes:
time: 1140 us
  waiting for transfers between devices  681 us (60%)
  blocking collectives  375 us (33%)
  matrix products  36.8 us (3%)
  local copies, waits for them, and re-layouts  20.4 us (2%)
  between operations  15 us (1%)
    unnamed x1, blocking collectives  375 us
    all_gather x1, waiting for transfers between devices, per_device(): lax.all_gather(tokens, 'mp', axis=0, tiled=True)  308 us
    all_gather x1, waiting for transfers between devices, per_device(): lax.all_gather(out_grad, 'mp', axis=0, tiled=True)  303 us
    all_gather x1, waiting for transfers between devices, per_device(): lax.all_gather(up_weight * up_keep, 'dp', axis=1, tiled=True)  26.5 us
  transfers between devices with their start and end apart: 8, of which 5 were waited for; matrix products, arithmetic and copies ran while one was open for 6% of the time, Pallas kernels for 0%

commit v1 on v0

v1 whole, which is shorter than its diff:
```python
import jax
import jax.numpy as jnp
from jax import lax
from jax.experimental import pallas as pl
from jax.experimental.pallas import tpu as pltpu
from jax.sharding import Mesh
from jax.sharding import PartitionSpec as P

BLK = 128
AXES = ("x_hi", "core", "x_lo", "y", "z")
SIZES = (2, 2, 2, 4, 8)
DP = ("x_hi", "core")
MP = ("x_lo", "y", "z")
N_X, N_Y, N_Z = 2, 4, 8
BF = jnp.bfloat16
F32 = jnp.float32
WHOLE = pl.BlockSpec(memory_space=pltpu.VMEM)
SCALARS = pl.BlockSpec(memory_space=pltpu.SMEM)


def call(kernel, out_shape, in_specs, bytes_accessed, flops=0, **more):
    return pl.pallas_call(
        kernel,
        out_shape=out_shape,
        in_specs=in_specs,
        compiler_params=pltpu.CompilerParams(vmem_limit_bytes=(8 << 20) + 2 * bytes_accessed),
        cost_estimate=pl.CostEstimate(
            flops=flops, bytes_accessed=bytes_accessed, transcendentals=0
        ),
        **more,
    )


def fetch(block, axis, offset):
    size = SIZES[AXES.index(axis)]
    return lax.ppermute(block, axis, [(i, (i - offset) % size) for i in range(size)])


def pack(arrays):
    own, width = arrays[0].shape
    tail, rows = width // (own - 1), own - 1

    def kernel(*refs):
        out = refs[-1]
        for k, ref in enumerate(refs[:-1]):
            out[k * rows : (k + 1) * rows, :width] = ref[:rows, :]
            for i in range(rows):
                spot = k * rows + i
                out[spot : spot + 1, width:] = ref[rows : rows + 1, i * tail : (i + 1) * tail]

    out = jax.ShapeDtypeStruct((rows * len(arrays), width + tail), BF)
    return call(kernel, out, [WHOLE] * len(arrays), 4 * own * width * len(arrays))(*arrays)


def by_array(mine, other):
    rows = mine.shape[0] // 2

    def kernel(mine_ref, other_ref, *out):
        for k in range(2):
            out[k][:rows, :] = mine_ref[k * rows : (k + 1) * rows, :]
            out[k][rows:, :] = other_ref[k * rows : (k + 1) * rows, :]

    out = [jax.ShapeDtypeStruct(mine.shape, BF)] * 2
    return call(kernel, out, [WHOLE] * 2, 4 * mine.shape[0] * mine.shape[1])(mine, other)


def stack(blocks):
    starts = [sum(b.shape[0] for b in blocks[:i]) for i in range(len(blocks) + 1)]

    def kernel(*refs):
        for ref, start in zip(refs[:-1], starts):
            refs[-1][start : start + ref.shape[0], :] = ref[...]

    whole = jax.ShapeDtypeStruct((starts[-1], blocks[0].shape[1]), blocks[0].dtype)
    size = 4 * starts[-1] * blocks[0].shape[1]
    return call(kernel, whole, [WHOLE] * len(blocks), size)(*blocks)


def beside(parts):
    rows, cols = parts[0].shape

    def kernel(left, right, out):
        out[:, :cols] = left[...]
        out[:, cols:] = right[...]

    out = jax.ShapeDtypeStruct((rows, 2 * cols), parts[0].dtype)
    return call(kernel, out, [WHOLE] * 2, 8 * rows * cols)(*parts)


def unpack(pieces, units, own, width):
    tail = width // (own - 1)
    flat = [block for _, blocks in pieces for block in blocks]

    def kernel(*refs):
        out, at = refs[-1], 0
        for firsts, blocks in pieces:
            held = refs[at : at + len(blocks)]
            at += len(blocks)
            for i, unit in enumerate(firsts):
                rows = slice(8 * i, 8 * i + 8)
                top = unit * own
                value = jnp.concatenate([ref[rows, :] for ref in held], axis=1)
                out[top : top + own - 1, :] = value[:, :width]
                for j in range(own - 1):
                    part = value[j : j + 1, width:]
                    out[top + own - 1 : top + own, j * tail : (j + 1) * tail] = part

    whole = jax.ShapeDtypeStruct((units * own, width), BF)
    return call(kernel, whole, [WHOLE] * len(flat), 4 * units * own * width)(*flat)


def mask_weights(weights, keep_rows):
    rows, cols = weights[0].shape
    panels = rows // BLK

    def kernel(keep_ref, *refs):
        for m in range(len(weights)):
            for p in range(panels):
                row = m * panels + p
                keep = keep_ref[row : row + 1, :]
                kept = refs[m][p * BLK : (p + 1) * BLK, :].astype(F32) * keep
                refs[-1][row * BLK : (row + 1) * BLK, :] = kept.astype(BF)

    out = jax.ShapeDtypeStruct((rows * len(weights), cols), BF)
    return call(kernel, out, [WHOLE] * 4, 12 * rows * cols)(keep_rows, *weights)


def project(place, rows_in, blocks, row_block, count):
    total, width = rows_in.shape
    cols = width // 4

    def kernel(place_ref, x_ref, *refs):
        out = refs[-1]
        for b in range(4):

            @pl.when(pl.program_id(0) == b)
            def _():
                part = lax.dot_general(
                    x_ref[...], refs[b][...], (((1,), (1,)), ((), ())), preferred_element_type=F32
                )
                out[...] = part if b == 0 else out[...] + part

    return pl.pallas_call(
        kernel,
        grid_spec=pltpu.PrefetchScalarGridSpec(
            num_scalar_prefetch=1,
            grid=(4,),
            in_specs=[pl.BlockSpec((total, cols), lambda j, place: (0, place[j]))]
            + [pl.BlockSpec((count, cols), lambda j, place: (row_block, 0))] * 4,
            out_specs=pl.BlockSpec((total, count), lambda j, place: (0, 0)),
        ),
        out_shape=jax.ShapeDtypeStruct((total, count), F32),
        compiler_params=pltpu.CompilerParams(vmem_limit_bytes=24 << 20),
        cost_estimate=pl.CostEstimate(
            flops=2 * total * count * width,
            bytes_accessed=2 * total * width + 2 * count * width + 4 * total * count,
            transcendentals=0,
        ),
    )(place, rows_in, *blocks)


def spread(grads, blocks):
    total, count = grads.shape
    cols, n = blocks[0].shape[1], len(blocks)

    def kernel(g_ref, *refs):
        for j in range(n):

            @pl.when(pl.program_id(0) == j)
            def _():
                part = jnp.dot(g_ref[...], refs[j][...], preferred_element_type=F32)
                refs[-1][...] = part.astype(BF)

    return pl.pallas_call(
        kernel,
        grid=(n,),
        in_specs=[pl.BlockSpec((total, count), lambda j: (0, 0))]
        + [pl.BlockSpec((count, cols), lambda j: (0, 0))] * n,
        out_specs=pl.BlockSpec((total, cols), lambda j: (0, j)),
        out_shape=jax.ShapeDtypeStruct((total, n * cols), BF),
        compiler_params=pltpu.CompilerParams(vmem_limit_bytes=24 << 20),
        cost_estimate=pl.CostEstimate(
            flops=2 * n * total * count * cols,
            bytes_accessed=2 * n * cols * (total + count),
            transcendentals=0,
        ),
    )(grads, *blocks)


def deal(total, unit):
    count = total.shape[0] // unit

    def kernel(ref, *out):
        for i in range(count):
            out[i][...] = ref[i * unit : (i + 1) * unit, :]

    spec = [jax.ShapeDtypeStruct((unit, total.shape[1]), BF)] * count
    return call(kernel, spec, [WHOLE], 6 * total.shape[0] * total.shape[1])(total)


def activations(z, pre, hidden_grad, unit):
    total, hid = hidden_grad.shape
    block = N_Y * unit

    def kernel(z_ref, pre_ref, grad_ref, first_ref, hidden_ref):
        for dz in range(N_Z):
            spot = lax.rem(z_ref[0] + dz, N_Z)
            gate_pre, up_pre = pre_ref[spot, :, :hid], pre_ref[spot, :, hid:]
            rows = [slice((dy * N_Z + dz) * unit, (dy * N_Z + dz + 1) * unit) for dy in range(N_Y)]
            grad = jnp.concatenate([grad_ref[r, :] for r in rows], axis=0)
            sigma = jax.nn.sigmoid(gate_pre)
            swish = gate_pre * sigma
            hidden = (swish * up_pre).astype(BF)
            up_grad = (grad * swish).astype(BF)
            gate_grad = (grad * up_pre * sigma * (1.0 + gate_pre * (1.0 - sigma))).astype(BF)
            first_ref[spot, :, :hid] = gate_grad
            first_ref[spot, :, hid:] = up_grad
            for dy in range(N_Y):
                part = slice(dy * unit, (dy + 1) * unit)
                hidden_ref[rows[dy], :] = hidden[part]

    out = [
        jax.ShapeDtypeStruct((N_Z, block, 2 * hid), BF),
        jax.ShapeDtypeStruct((total, hid), BF),
    ]
    first, hidden = call(kernel, out, [SCALARS] + [WHOLE] * 2, 16 * total * hid)(
        z, pre.reshape(N_Z, block, 2 * hid), hidden_grad
    )
    return first.reshape(total, 2 * hid), hidden


def weight_grads(order, left, right):
    tokens, hid = left.shape
    cols = right.shape[1] // 4

    def kernel(order_ref, left_ref, right_ref, give_ref, keep_ref):
        part = lax.dot_general(
            left_ref[...], right_ref[...], (((0,), (0,)), ((), ())), preferred_element_type=F32
        )

        @pl.when(pl.program_id(0) < 2)
        def _():
            give_ref[0] = part.astype(BF)

        @pl.when(pl.program_id(0) >= 2)
        def _():
            keep_ref[0] = part

    return pl.pallas_call(
        kernel,
        grid_spec=pltpu.PrefetchScalarGridSpec(
            num_scalar_prefetch=1,
            grid=(4,),
            in_specs=[
                pl.BlockSpec((tokens, hid), lambda j, order: (0, 0)),
                pl.BlockSpec((tokens, cols), lambda j, order: (0, order[j])),
            ],
            out_specs=[
                pl.BlockSpec((1, hid, cols), lambda j, order: (jnp.minimum(j, 1), 0, 0)),
                pl.BlockSpec((1, hid, cols), lambda j, order: (jnp.maximum(j - 2, 0), 0, 0)),
            ],
        ),
        out_shape=[
            jax.ShapeDtypeStruct((2, hid, cols), BF),
            jax.ShapeDtypeStruct((2, hid, cols), F32),
        ],
        compiler_params=pltpu.CompilerParams(vmem_limit_bytes=24 << 20),
        cost_estimate=pl.CostEstimate(
            flops=8 * tokens * hid * cols,
            bytes_accessed=12 * hid * cols + 8 * tokens * cols,
            transcendentals=0,
        ),
    )(order, left, right)


def per_device(tokens, out_grad, gate_weight, up_weight, down_weight, block_mask, assignment):
    own, width = tokens.shape
    hid, cols = gate_weight.shape
    panels, col_blocks = hid // BLK, cols // BLK
    unit = 2 * own
    x_hi, core, z = (lax.axis_index(a) for a in ("x_hi", "core", "z"))
    place = jnp.stack(
        [2 * x_hi + core, 2 * (1 - x_hi) + core, 2 * x_hi + 1 - core, 2 * (1 - x_hi) + 1 - core]
    )
    tie = lax.optimization_barrier

    panel_ids = lax.broadcasted_iota(jnp.int32, (panels, block_mask.shape[1]), 1)
    selector = (assignment[:, None] == panel_ids).astype(F32)
    slot_mask = jnp.einsum("sp,mpb->msb", selector, block_mask.astype(F32))
    slot_mask = lax.dynamic_slice_in_dim(slot_mask, place[0] * col_blocks, col_blocks, 2)
    keep = jnp.repeat(slot_mask, BLK, axis=2)

    mine = pack([tokens, out_grad])
    tok16, grd16 = by_array(mine, fetch(mine, "x_lo", 1))
    kept = mask_weights([gate_weight, up_weight, down_weight], keep.reshape(-1, cols))
    tok16, grd16, kept = tie((tok16, grd16, kept))

    away = fetch(kept, "x_hi", 1)
    z1, z7 = fetch(grd16, "z", 1), fetch(grd16, "z", -1)
    t1, t3, t2 = fetch(tok16, "y", 1), fetch(tok16, "y", -1), fetch(tok16, "y", 2)
    z1, z7, t1, t3, t2 = tie((z1, z7, t1, t3, t2))
    tok = unpack(
        [([2 * dy, 2 * dy + 1], [t]) for dy, t in enumerate((tok16, t1, t2, t3))], N_X * N_Y, own, width
    )
    tok = lax.all_gather(tok, "z", axis=0, tiled=True)
    near = stack([grd16, z1, z7])
    z2, z6, n1, n3 = tie(
        (fetch(z1, "z", 1), fetch(z7, "z", -1), fetch(near, "y", 1), fetch(near, "y", -1))
    )
    cut = near.shape[1] // 2
    z3, z5, n2a, n2b = tie(
        (
            fetch(z2, "z", 1),
            fetch(z6, "z", -1),
            fetch(n1[:, :cut], "y", 1),
            fetch(n3[:, cut:], "y", -1),
        )
    )
    z4 = beside(tie((fetch(z3[:, :cut], "z", 1), fetch(z5[:, cut:], "z", -1))))
    rest = stack([z2, z3, z4, z5, z6])
    r1, r3, away = tie((fetch(rest, "y", 1), fetch(rest, "y", -1), away))
    beside_kept, beside_away = fetch(kept, "core", 1), fetch(away, "core", 1)
    r2a, r2b = fetch(r1[:, :cut], "y", 1), fetch(r3[:, cut:], "y", -1)
    pieces = []
    for dy, n, r in ((0, [near], [rest]), (1, [n1], [r1]), (2, [n2a, n2b], [r2a, r2b]), (3, [n3], [r3])):
        for offsets, blocks in (((0, 1, 7), n), ((2, 3, 4, 5, 6), r)):
            pieces.append(([2 * (N_Z * dy + dz) + dx for dz in offsets for dx in range(N_X)], blocks))
    grd = unpack(pieces, N_X * N_Y * N_Z, own, width)

    blocks = [kept, away, beside_kept, beside_away]
    hidden_grad = project(place, grd, blocks, 2, hid)
    pre = project(place, tok, blocks, 0, 2 * hid)
    by_z, hidden = activations(z[None], pre, hidden_grad, unit)

    total = spread(by_z, blocks)
    total = lax.psum_scatter(total, "z", scatter_dimension=0, tiled=True)
    order = place[::-1]
    give_b, keep_b = weight_grads(order, hidden, grd)
    give_b = fetch(give_b, "core", 1)
    give_a, keep_a = weight_grads(order, by_z, tok)
    give_a, give_b, keep_a = tie((give_a, give_b, keep_a))
    sums_b = keep_b + give_b.astype(F32)
    far_b = fetch(sums_b[0].astype(BF), "x_hi", 1)
    sums_a = keep_a + fetch(give_a, "core", 1).astype(F32)
    far_a = fetch(sums_a[0].astype(BF), "x_hi", 1)

    parts = deal(total, unit)
    parts = [parts[0]] + [fetch(parts[dy], "y", -dy) for dy in range(1, N_Y)]
    both = sum(part.astype(F32) for part in parts)
    both = both[:own] + fetch(both[own:].astype(BF), "x_lo", 1).astype(F32)
    quarters = [both[:, i * cols : (i + 1) * cols] for i in (0, 2, 1, 3)]
    quarters = [jnp.where(core == 0, quarters[i], quarters[i ^ 1]) for i in range(4)]
    quarters = [jnp.where(x_hi == 0, quarters[i], quarters[i ^ 2]) for i in range(4)]
    input_grad = jnp.concatenate(quarters, axis=1).astype(BF)

    def finish(sums, far, rows):
        total = (sums[1] + far.astype(F32)).reshape(-1, panels, BLK, cols)
        return (total * rows[:, :, None, :]).astype(BF).reshape(-1, hid, cols)

    gate_up_grad = finish(sums_a, far_a, keep[:2])
    down_grad = finish(sums_b, far_b, keep[2:])
    return (input_grad, gate_up_grad[0], gate_up_grad[1], down_grad[0])


def solution(mesh):
    fine = Mesh(mesh.devices.reshape(SIZES), AXES)
    rows = P(DP + MP, None)
    weights = P(MP, DP)
    return jax.shard_map(
        per_device,
        mesh=fine,
        in_specs=(rows, rows, weights, weights, weights, P(), P(MP)),
        out_specs=(rows, weights, weights, weights),
        check_vma=False,
    )
```

time: 1140 us -> 227 us (0.20)
  waiting for transfers between devices: 681 us -> 89.1 us
  blocking collectives: 375 us -> 0 us
  starting transfers between devices: 0.5 us -> 48.8 us
  matrix products: 36.8 us -> 0.97 us
  Pallas kernels: 0 us -> 28.3 us
  local copies, waits for them, and re-layouts: 20.4 us -> 36.6 us
    all_gather x5 -> x1, waiting for transfers between devices: 680 us -> 0.01 us  [per_device(): tok = lax.all_gather(tok, 'z', axis=0, tiled=True)]
    unnamed x1 -> x0, blocking collectives: 375 us -> none
    ppermute x0 -> x31, waiting for transfers between devices: none -> 89.1 us  [fetch(): lax.ppermute(block, axis, [(i, (i - offset) % size) for i in range(size)])]
    ppermute x0 -> x31, starting transfers between devices: none -> 48.8 us  [fetch(): lax.ppermute(block, axis, [(i, (i - offset) % size) for i in range(size)])]
    dot_general x9 -> x1, matrix products: 36.8 us -> 0.97 us  [per_device(): slot_mask = jnp.einsum('sp,mpb->msb', selector, block_mask.astype(F32))]
    pallas_call x0 -> x15, Pallas kernels: none -> 28.3 us  [the longest x2 9.87 us: project(): pl.pallas_call(kernel, grid_spec=pltpu.PrefetchScalarGridSpec(num_scalar_...]
    unnamed x15 -> x71, local copies, waits for them, and re-layouts: 17.7 us -> 31.4 us
  transfers between devices with their start and end apart: 8 -> 33, of which waited for: 5 -> 14; matrix products, arithmetic and copies ran while one was open for 6% -> 5% of each run, Pallas kernels for 0% -> 7%
where the time goes in v1:
time: 227 us; the launch traced here: 225 us
  waiting for transfers between devices  89.1 us (39%)
  starting transfers between devices  48.8 us (21%)
  local copies, waits for them, and re-layouts  36.6 us (16%)
  Pallas kernels  28.3 us (12%)
  between operations  14.4 us (6%)
  other arithmetic  6.36 us (3%)
    ppermute x31, waiting for transfers between devices, fetch(): lax.ppermute(block, axis, [(i, (i - offset) % size) for i in range(size)])  89.1 us
    ppermute x31, starting transfers between devices, fetch(): lax.ppermute(block, axis, [(i, (i - offset) % size) for i in range(size)])  48.8 us
    unnamed x71, local copies, waits for them, and re-layouts  31.4 us
    pallas_call x2, Pallas kernels, project(): pl.pallas_call(kernel, grid_spec=pltpu.PrefetchScalarGridSpec(num_scalar_...  9.87 us
    pallas_call x2, Pallas kernels, weight_grads(): pl.pallas_call(kernel, grid_spec=pltpu.PrefetchScalarGridSpec(num_scalar_...  9.05 us
    pallas_call x1, Pallas kernels, spread(): pl.pallas_call(kernel, grid=(n,), in_specs=[pl.BlockSpec((total, count),...  5.09 us
  transfers between devices with their start and end apart: 33, of which 14 were waited for; matrix products, arithmetic and copies ran while one was open for 5% of the time, Pallas kernels for 7%

profile of v1, /device:TPU:2, one launch (start us, length us, event | category | flops | bytes accessed | tf_op | source)
XLA Modules:
  0.0 224.6 jit_solution(18315294185423750825)
XLA Ops:
  9.1 2.4 %collective-permute-start = (bf16[16,4608]{1,0:T(8,128)(2,1)S(1)}, bf16[16,4608]{1,0:T(8,128)(2,1)S(1)}, u32[]{:S(2)}, u32[]{:S(2)}) collective-permute-start(bf16[16,4608]{1,0:T(8,128)(2,1)S(1)} %shard_map.102.mine_ref), channel_id=1, source_target_pairs={{0,32},{32,0},{1,33},{33,1},{2,34},{34,2},{3,35},{35,3},{4,36},{36... | collective-permute-start | bytes 442376 | tf_op jit(solution)/shard_map/ppermute | solution.py:36
  16.8 4.0 %collective-permute-start.1 = (bf16[16,4608]{1,0:T(8,128)(2,1)S(1)}, bf16[16,4608]{1,0:T(8,128)(2,1)S(1)}, u32[]{:S(2)}, u32[]{:S(2)}) collective-permute-start(bf16[16,4608]{1,0:T(8,128)(2,1)S(1)} %get-tuple-element.43.refs_0_), channel_id=1, source_target_pairs={{0,7},{1,0},{2,1},{3,2},{4,3},{5,4},{6,5},{7,6},{8,15},{9,8},{10,9... | collective-permute-start | bytes 442376 | tf_op jit(solution)/shard_map/ppermute | solution.py:36
  21.4 3.2 %collective-permute-start.5 = (bf16[16,4608]{1,0:T(8,128)(2,1)S(1)}, bf16[16,4608]{1,0:T(8,128)(2,1)S(1)}, u32[]{:S(2)}, u32[]{:S(2)}) collective-permute-start(bf16[16,4608]{1,0:T(8,128)(2,1)S(1)} %get-tuple-element.42.refs_0_), channel_id=1, source_target_pairs={{0,16},{8,24},{16,0},{24,8},{1,17},{9,25},{17,1},{25,9},{2,18},{10... | collective-permute-start | bytes 442376 | tf_op jit(solution)/shard_map/ppermute | solution.py:36
  25.3 2.6 %collective-permute-start.3 = (bf16[16,4608]{1,0:T(8,128)(2,1)S(1)}, bf16[16,4608]{1,0:T(8,128)(2,1)S(1)}, u32[]{:S(2)}, u32[]{:S(2)}) collective-permute-start(bf16[16,4608]{1,0:T(8,128)(2,1)S(1)} %get-tuple-element.42.refs_0_), channel_id=1, source_target_pairs={{0,24},{8,0},{16,8},{24,16},{1,25},{9,1},{17,9},{25,17},{2,26},{10... | collective-permute-start | bytes 442376 | tf_op jit(solution)/shard_map/ppermute | solution.py:36
  27.9 1.6 collective-permute-done.5.refs_2_
  29.5 2.0 collective-permute-done.4.refs_3_
  32.6 2.3 %collective-permute-start.18 = (bf16[768,1024]{1,0:T(8,128)(2,1)S(1)}, bf16[768,1024]{1,0:T(8,128)(2,1)S(1)}, u32[]{:S(2)}, u32[]{:S(2)}) collective-permute-start(bf16[768,1024]{1,0:T(8,128)(2,1)S(1)} %shard_map.104.refs_0_), channel_id=1, source_target_pairs={{0,128},{128,0},{1,129},{129,1},{2,130},{130,2},{3,131},{131,3},{4... | collective-permute-start | bytes 4718600 | tf_op jit(solution)/shard_map/ppermute | solution.py:36
  35.9 1.2 collective-permute-start.9
  37.0 2.2 collective-permute-start.8
  39.9 1.8 collective-permute-start.6
  42.0 3.1 %collective-permute-done.6.refs_0_ = bf16[16,4608]{1,0:T(8,128)(2,1)S(1)} collective-permute-done((bf16[16,4608]{1,0:T(8,128)(2,1)S(1)}, bf16[16,4608]{1,0:T(8,128)(2,1)S(1)}, u32[]{:S(2)}, u32[]{:S(2)}) %collective-permute-start.6) | collective-permute-done | bytes 147488 | tf_op jit(solution)/shard_map/ppermute | solution.py:36
  45.1 3.2 %collective-permute-done.7.refs_4_ = bf16[16,4608]{1,0:T(8,128)(2,1)S(1)} collective-permute-done((bf16[16,4608]{1,0:T(8,128)(2,1)S(1)}, bf16[16,4608]{1,0:T(8,128)(2,1)S(1)}, u32[]{:S(2)}, u32[]{:S(2)}) %collective-permute-start.7) | collective-permute-done | bytes 147488 | tf_op jit(solution)/shard_map/ppermute | solution.py:36
  49.2 2.5 %collective-permute-start.12 = (bf16[48,2304]{1,0:T(8,128)(2,1)S(1)}, bf16[48,2304]{1,0:T(8,128)(2,1)S(1)}, u32[]{:S(2)}, u32[]{:S(2)}) collective-permute-start(bf16[48,2304]{1,0:T(8,128)(2,1)S(1)} %slice.71), channel_id=1, source_target_pairs={{0,24},{8,0},{16,8},{24,16},{1,25},{9,1},{17,9},{25,17},{2,26},{10... | collective-permute-start | bytes 663560 | tf_op jit(solution)/shard_map/ppermute | solution.py:36
  51.7 1.3 collective-permute-start.10
  53.7 6.4 %collective-permute-done.10.refs_1_ = bf16[16,4608]{1,0:T(8,128)(2,1)S(1)} collective-permute-done((bf16[16,4608]{1,0:T(8,128)(2,1)S(1)}, bf16[16,4608]{1,0:T(8,128)(2,1)S(1)}, u32[]{:S(2)}, u32[]{:S(2)}) %collective-permute-start.10) | collective-permute-done | bytes 147488 | tf_op jit(solution)/shard_map/ppermute | solution.py:36
  60.1 2.5 %collective-permute-done.11.refs_3_ = bf16[16,4608]{1,0:T(8,128)(2,1)S(1)} collective-permute-done((bf16[16,4608]{1,0:T(8,128)(2,1)S(1)}, bf16[16,4608]{1,0:T(8,128)(2,1)S(1)}, u32[]{:S(2)}, u32[]{:S(2)}) %collective-permute-start.11) | collective-permute-done | bytes 147488 | tf_op jit(solution)/shard_map/ppermute | solution.py:36
  63.7 3.2 %collective-permute-start.14 = (bf16[16,2304]{1,0:T(8,128)(2,1)S(1)}, bf16[16,2304]{1,0:T(8,128)(2,1)S(1)}, u32[]{:S(2)}, u32[]{:S(2)}) collective-permute-start(bf16[16,2304]{1,0:T(8,128)(2,1)S(1)} %slice.73), channel_id=1, source_target_pairs={{0,7},{1,0},{2,1},{3,2},{4,3},{5,4},{6,5},{7,6},{8,15},{9,8},{10,9... | collective-permute-start | bytes 221192 | tf_op jit(solution)/shard_map/ppermute | solution.py:36
  66.9 3.9 %collective-permute-done.15.right = bf16[16,2304]{1,0:T(8,128)(2,1)S(1)} collective-permute-done((bf16[16,2304]{1,0:T(8,128)(2,1)S(1)}, bf16[16,2304]{1,0:T(8,128)(2,1)S(1)}, u32[]{:S(2)}, u32[]{:S(2)}) %collective-permute-start.15) | collective-permute-done | bytes 73760 | tf_op jit(solution)/shard_map/ppermute | solution.py:36
  71.0 3.2 %collective-permute-start.16 = (bf16[80,4608]{1,0:T(8,128)(2,1)S(1)}, bf16[80,4608]{1,0:T(8,128)(2,1)S(1)}, u32[]{:S(2)}, u32[]{:S(2)}) collective-permute-start(bf16[80,4608]{1,0:T(8,128)(2,1)S(1)} %shard_map.108.refs_1_), channel_id=1, source_target_pairs={{0,24},{8,0},{16,8},{24,16},{1,25},{9,1},{17,9},{25,17},{2,26},{10... | collective-permute-start | bytes 2211848 | tf_op jit(solution)/shard_map/ppermute | solution.py:36
  75.1 10.8 %collective-permute-done.17.refs_9_ = bf16[80,4608]{1,0:T(8,128)(2,1)S(1)} collective-permute-done((bf16[80,4608]{1,0:T(8,128)(2,1)S(1)}, bf16[80,4608]{1,0:T(8,128)(2,1)S(1)}, u32[]{:S(2)}, u32[]{:S(2)}) %collective-permute-start.17) | collective-permute-done | bytes 737312 | tf_op jit(solution)/shard_map/ppermute | solution.py:36
  87.6 3.2 %collective-permute-start.21 = (bf16[80,2304]{1,0:T(8,128)(2,1)}, bf16[80,2304]{1,0:T(8,128)(2,1)}, u32[]{:S(2)}, u32[]{:S(2)}) collective-permute-start(bf16[80,2304]{1,0:T(8,128)(2,1)} %slice.75), channel_id=1, source_target_pairs={{0,24},{8,0},{16,8},{24,16},{1,25},{9,1},{17,9},{25,17},{2,26},{10... | collective-permute-start | bytes 1105928 | tf_op jit(solution)/shard_map/ppermute | solution.py:36
  91.0 9.0 %collective-permute-done.22.refs_7_ = bf16[80,2304]{1,0:T(8,128)(2,1)S(1)} collective-permute-done((bf16[80,2304]{1,0:T(8,128)(2,1)}, bf16[80,2304]{1,0:T(8,128)(2,1)S(1)}, u32[]{:S(2)}, u32[]{:S(2)}) %collective-permute-start.22) | collective-permute-done | bytes 368672 | tf_op jit(solution)/shard_map/ppermute | solution.py:36
  99.9 1.1 copy-done.6
  102.0 1.1 copy-done.12
  103.2 1.1 copy-done.14
  108.2 2.4 %shard_map.110.x_ref.right_ref = bf16[576,4096]{1,0:T(8,128)(2,1)S(1)} custom-call(bf16[48,4608]{1,0:T(8,128)(2,1)S(1)} %copy-done.10, bf16[80,4608]{1,0:T(8,128)(2,1)S(1)} %copy-done.6, bf16[48,4608]{1,0:T(8,128)(2,1)S(1)} %copy-done.18, bf16[80,4608]{1,0:T(8,128)(2,1)S(1)} %copy-done.14, bf16[48,2304]{1,0:T(8,128)(2,1)S(1)} %copy-done.28, ...), custom_call_target="tpu_custom_call" | custom-call | bytes 9437184 | tf_op jit(solution)/shard_map/pallas_call | solution.py:109
  110.6 4.2 %shard_map.111.grad_ref = f32[576,256]{1,0:T(8,128)S(1)} custom-call(s32[4]{0:T(128)S(1)} %pad_add_fusion.place_ref, bf16[576,4096]{1,0:T(8,128)(2,1)S(1)} %shard_map.110.x_ref.right_ref, bf16[768,1024]{1,0:T(8,128)(2,1)S(1)} %shard_map.104.refs_0_, bf16[768,1024]{1,0:T(8,128)(2,1)S(1)} %collective-permute-done.18.refs_1_, ...), custom_call_target="tpu_custom_call" | custom-call | flops 1207959552 | bytes 7405568 | tf_op jit(solution)/shard_map/pallas_call | solution.py:143
  114.8 2.2 copy-done
  117.8 2.3 %copy-done.3 = bf16[576,4096]{1,0:T(8,128)(2,1)S(1)} copy-done((bf16[576,4096]{1,0:T(8,128)(2,1)S(1)}, bf16[576,4096]{1,0:T(8,128)(2,1)}, u32[]{:S(2)}) %copy-start.3) | copy-done | bytes 4718616
  120.2 5.7 %shard_map.109 = f32[576,512]{1,0:T(8,128)S(1)} custom-call(s32[4]{0:T(128)S(1)} %pad_add_fusion.place_ref, bf16[576,4096]{1,0:T(8,128)(2,1)S(1)} %copy-done.3, bf16[768,1024]{1,0:T(8,128)(2,1)S(1)} %shard_map.104.refs_0_, bf16[768,1024]{1,0:T(8,128)(2,1)S(1)} %collective-permute-done.18.refs_1_, bf16[768,1024]{1,0:T(8,128)(2,1)} %collective-permute-done.19.refs_2_, ...), custom_call_target="tpu_custom_call" | custom-call | flops 2415919104 | bytes 10092544 | tf_op jit(solution)/shard_map/pallas_call | solution.py:143
  126.2 5.1 %shard_map.113 = bf16[576,4096]{1,0:T(8,128)(2,1)S(1)} custom-call(bf16[576,512]{1,0:T(8,128)(2,1)S(1)} %bitcast.48, bf16[768,1024]{1,0:T(8,128)(2,1)S(1)} %shard_map.104.refs_0_, bf16[768,1024]{1,0:T(8,128)(2,1)S(1)} %collective-permute-done.18.refs_1_, bf16[768,1024]{1,0:T(8,128)(2,1)} %collective-permute-done.19.refs_2_, ...), custom_call_target="tpu_custom_call" | custom-call | flops 2415919104 | bytes 8912896 | tf_op jit(solution)/shard_map/pallas_call | solution.py:174
  131.4 2.2 copy-done.2
  134.5 2.3 %copy-done.1 = bf16[576,4096]{1,0:T(8,128)(2,1)S(1)} copy-done((bf16[576,4096]{1,0:T(8,128)(2,1)S(1)}, bf16[576,4096]{1,0:T(8,128)(2,1)}, u32[]{:S(2)}) %copy-start.1) | copy-done | bytes 4718616
  136.8 3.6 %shard_map.116 = (bf16[2,256,1024]{2,1,0:T(8,128)(2,1)S(1)}, f32[2,256,1024]{2,1,0:T(8,128)S(1)}) custom-call(s32[4]{0:T(128)S(1)} %rev.3.order_ref, bf16[576,256]{1,0:T(8,128)(2,1)S(1)} %get-tuple-element.69.left_ref, bf16[576,4096]{1,0:T(8,128)(2,1)S(1)} %copy-done.1), custom_call_target="tpu_custom_call" | custom-call | flops 1207959552 | bytes 7864320 | tf_op jit(solution)/shard_map/pallas_call | solution.py:249
  140.5 2.3 %copy-done.4 = bf16[576,4096]{1,0:T(8,128)(2,1)S(1)} copy-done((bf16[576,4096]{1,0:T(8,128)(2,1)S(1)}, bf16[576,4096]{1,0:T(8,128)(2,1)}, u32[]{:S(2)}) %copy-start.4) | copy-done | bytes 4718616
  142.9 5.5 %shard_map.115 = (bf16[2,512,1024]{2,1,0:T(8,128)(2,1)S(1)}, f32[2,512,1024]{2,1,0:T(8,128)S(1)}) custom-call(s32[4]{0:T(128)S(1)} %rev.3.order_ref, bf16[576,512]{1,0:T(8,128)(2,1)S(1)} %bitcast.49, bf16[576,4096]{1,0:T(8,128)(2,1)S(1)} %copy-done.4), custom_call_target="tpu_custom_call" | custom-call | flops 2415919104 | bytes 11010048 | tf_op jit(solution)/shard_map/pallas_call | solution.py:249
  148.9 3.8 %collective-permute-done.28 = bf16[2,512,1024]{2,1,0:T(8,128)(2,1)S(1)} collective-permute-done((bf16[2,512,1024]{2,1,0:T(8,128)(2,1)S(1)}, bf16[2,512,1024]{2,1,0:T(8,128)(2,1)S(1)}, u32[]{:S(2)}, u32[]{:S(2)}) %collective-permute-start.28) | collective-permute-done | bytes 2097184 | tf_op jit(solution)/shard_map/ppermute | solution.py:36
  153.8 1.3 fusion.1
  157.3 2.5 %collective-permute-start.30 = (bf16[256,1024]{1,0:T(8,128)(2,1)}, bf16[256,1024]{1,0:T(8,128)(2,1)}, u32[]{:S(2)}, u32[]{:S(2)}) collective-permute-start(bf16[256,1024]{1,0:T(8,128)(2,1)} %fusion.5), channel_id=1, source_target_pairs={{0,128},{128,0},{1,129},{129,1},{2,130},{130,2},{3,131},{131,3},{4... | collective-permute-start | bytes 1572872 | tf_op jit(solution)/shard_map/ppermute | solution.py:36
  160.0 33.6 %collective-permute-done.30 = bf16[256,1024]{1,0:T(8,128)(2,1)} collective-permute-done((bf16[256,1024]{1,0:T(8,128)(2,1)}, bf16[256,1024]{1,0:T(8,128)(2,1)}, u32[]{:S(2)}, u32[]{:S(2)}) %collective-permute-start.30) | collective-permute-done | bytes 524320 | tf_op jit(solution)/shard_map/ppermute | solution.py:36
  193.6 2.0 fusion.4
  195.6 1.9 fusion
  198.6 1.2 collective-permute-start.23
  199.9 3.4 %collective-permute-start.24 = (bf16[18,4096]{1,0:T(8,128)(2,1)S(1)}, bf16[18,4096]{1,0:T(8,128)(2,1)S(1)}, u32[]{:S(2)}, u32[]{:S(2)}) collective-permute-start(bf16[18,4096]{1,0:T(8,128)(2,1)S(1)} %get-tuple-element.66), channel_id=1, source_target_pairs={{0,16},{8,24},{16,0},{24,8},{1,17},{9,25},{17,1},{25,9},{2,18},{10... | collective-permute-start | bytes 442376 | tf_op jit(solution)/shard_map/ppermute | solution.py:36
  204.5 2.1 collective-permute-done.23
  206.7 5.1 %collective-permute-done.24 = bf16[18,4096]{1,0:T(8,128)(2,1)S(1)} collective-permute-done((bf16[18,4096]{1,0:T(8,128)(2,1)S(1)}, bf16[18,4096]{1,0:T(8,128)(2,1)S(1)}, u32[]{:S(2)}, u32[]{:S(2)}) %collective-permute-start.24) | collective-permute-done | bytes 147488 | tf_op jit(solution)/shard_map/ppermute | solution.py:36
  211.9 2.2 collective-permute-start.26
  215.1 1.9 collective-permute-done.26
  (134 shorter events, 32.5 us)
Async XLA Ops:
  7.2 110.7 %all-gather.2.cloned.1.call-start = ((), (), s32[]{:S(2)}) async-start(), calls=%async_computation.1 | async-start | bytes 5308416 | tf_op jit(solution)/shard_map/all_gather | solution.py:305
  9.1 6.9 %collective-permute-start = (bf16[16,4608]{1,0:T(8,128)(2,1)S(1)}, bf16[16,4608]{1,0:T(8,128)(2,1)S(1)}, u32[]{:S(2)}, u32[]{:S(2)}) collective-permute-start(bf16[16,4608]{1,0:T(8,128)(2,1)S(1)} %shard_map.102.mine_ref), channel_id=1, source_target_pairs={{0,32},{32,0},{1,33},{33,1},{2,34},{34,2},{3,35},{35,3},{4,36},{36... | collective-permute-start | bytes 442376 | tf_op jit(solution)/shard_map/ppermute | solution.py:36
  16.0 11.9 %collective-permute-start.2 = (bf16[16,4608]{1,0:T(8,128)(2,1)S(1)}, bf16[16,4608]{1,0:T(8,128)(2,1)S(1)}, u32[]{:S(2)}, u32[]{:S(2)}) collective-permute-start(bf16[16,4608]{1,0:T(8,128)(2,1)S(1)} %get-tuple-element.43.refs_0_), channel_id=1, source_target_pairs={{0,1},{1,2},{2,3},{3,4},{4,5},{5,6},{6,7},{7,0},{8,9},{9,10},{10,1... | collective-permute-start | bytes 442376 | tf_op jit(solution)/shard_map/ppermute | solution.py:36
  16.8 11.1 %collective-permute-start.1 = (bf16[16,4608]{1,0:T(8,128)(2,1)S(1)}, bf16[16,4608]{1,0:T(8,128)(2,1)S(1)}, u32[]{:S(2)}, u32[]{:S(2)}) collective-permute-start(bf16[16,4608]{1,0:T(8,128)(2,1)S(1)} %get-tuple-element.43.refs_0_), channel_id=1, source_target_pairs={{0,7},{1,0},{2,1},{3,2},{4,3},{5,4},{6,5},{7,6},{8,15},{9,8},{10,9... | collective-permute-start | bytes 442376 | tf_op jit(solution)/shard_map/ppermute | solution.py:36
  21.4 8.1 %collective-permute-start.5 = (bf16[16,4608]{1,0:T(8,128)(2,1)S(1)}, bf16[16,4608]{1,0:T(8,128)(2,1)S(1)}, u32[]{:S(2)}, u32[]{:S(2)}) collective-permute-start(bf16[16,4608]{1,0:T(8,128)(2,1)S(1)} %get-tuple-element.42.refs_0_), channel_id=1, source_target_pairs={{0,16},{8,24},{16,0},{24,8},{1,17},{9,25},{17,1},{25,9},{2,18},{10... | collective-permute-start | bytes 442376 | tf_op jit(solution)/shard_map/ppermute | solution.py:36
  24.6 6.8 %collective-permute-start.4 = (bf16[16,4608]{1,0:T(8,128)(2,1)S(1)}, bf16[16,4608]{1,0:T(8,128)(2,1)S(1)}, u32[]{:S(2)}, u32[]{:S(2)}) collective-permute-start(bf16[16,4608]{1,0:T(8,128)(2,1)S(1)} %get-tuple-element.42.refs_0_), channel_id=1, source_target_pairs={{0,8},{8,16},{16,24},{24,0},{1,9},{9,17},{17,25},{25,1},{2,10},{10... | collective-permute-start | bytes 442376 | tf_op jit(solution)/shard_map/ppermute | solution.py:36
  25.3 6.2 %collective-permute-start.3 = (bf16[16,4608]{1,0:T(8,128)(2,1)S(1)}, bf16[16,4608]{1,0:T(8,128)(2,1)S(1)}, u32[]{:S(2)}, u32[]{:S(2)}) collective-permute-start(bf16[16,4608]{1,0:T(8,128)(2,1)S(1)} %get-tuple-element.42.refs_0_), channel_id=1, source_target_pairs={{0,24},{8,0},{16,8},{24,16},{1,25},{9,1},{17,9},{25,17},{2,26},{10... | collective-permute-start | bytes 442376 | tf_op jit(solution)/shard_map/ppermute | solution.py:36
  32.5 164.9 %reduce-scatter.2.cloned.1.call-start = ((), (), s32[]{:S(2)}) async-start(), calls=%async_computation.2 | async-start | bytes 5308416 | tf_op jit(solution)/shard_map/reduce_scatter | solution.py:336
  32.6 42.5 %collective-permute-start.18 = (bf16[768,1024]{1,0:T(8,128)(2,1)S(1)}, bf16[768,1024]{1,0:T(8,128)(2,1)S(1)}, u32[]{:S(2)}, u32[]{:S(2)}) collective-permute-start(bf16[768,1024]{1,0:T(8,128)(2,1)S(1)} %shard_map.104.refs_0_), channel_id=1, source_target_pairs={{0,128},{128,0},{1,129},{129,1},{2,130},{130,2},{3,131},{131,3},{4... | collective-permute-start | bytes 4718600 | tf_op jit(solution)/shard_map/ppermute | solution.py:36
  35.9 12.4 %collective-permute-start.9 = (bf16[48,4608]{1,0:T(8,128)(2,1)S(1)}, bf16[48,4608]{1,0:T(8,128)(2,1)S(1)}, u32[]{:S(2)}, u32[]{:S(2)}) collective-permute-start(bf16[48,4608]{1,0:T(8,128)(2,1)S(1)} %shard_map.106.refs_0_), channel_id=1, source_target_pairs={{0,8},{8,16},{16,24},{24,0},{1,9},{9,17},{17,25},{25,1},{2,10},{10... | collective-permute-start | bytes 1327112 | tf_op jit(solution)/shard_map/ppermute | solution.py:36
  37.0 11.3 %collective-permute-start.8 = (bf16[48,4608]{1,0:T(8,128)(2,1)S(1)}, bf16[48,4608]{1,0:T(8,128)(2,1)S(1)}, u32[]{:S(2)}, u32[]{:S(2)}) collective-permute-start(bf16[48,4608]{1,0:T(8,128)(2,1)S(1)} %shard_map.106.refs_0_), channel_id=1, source_target_pairs={{0,24},{8,0},{16,8},{24,16},{1,25},{9,1},{17,9},{25,17},{2,26},{10... | collective-permute-start | bytes 1327112 | tf_op jit(solution)/shard_map/ppermute | solution.py:36
  39.9 5.1 %collective-permute-start.6 = (bf16[16,4608]{1,0:T(8,128)(2,1)S(1)}, bf16[16,4608]{1,0:T(8,128)(2,1)S(1)}, u32[]{:S(2)}, u32[]{:S(2)}) collective-permute-start(bf16[16,4608]{1,0:T(8,128)(2,1)S(1)} %collective-permute-done.1.refs_1_), channel_id=1, source_target_pairs={{0,7},{1,0},{2,1},{3,2},{4,3},{5,4},{6,5},{7,6},{8,15},{9,8},{10,9... | collective-permute-start | bytes 442376 | tf_op jit(solution)/shard_map/ppermute | solution.py:36
  41.8 6.5 %collective-permute-start.7 = (bf16[16,4608]{1,0:T(8,128)(2,1)S(1)}, bf16[16,4608]{1,0:T(8,128)(2,1)S(1)}, u32[]{:S(2)}, u32[]{:S(2)}) collective-permute-start(bf16[16,4608]{1,0:T(8,128)(2,1)S(1)} %collective-permute-done.2.refs_2_), channel_id=1, source_target_pairs={{0,1},{1,2},{2,3},{3,4},{4,5},{5,6},{6,7},{7,0},{8,9},{9,10},{10,1... | collective-permute-start | bytes 442376 | tf_op jit(solution)/shard_map/ppermute | solution.py:36
  48.3 22.5 %copy-start.15 = (bf16[48,4608]{1,0:T(8,128)(2,1)}, bf16[48,4608]{1,0:T(8,128)(2,1)S(1)}, u32[]{:S(2)}) copy-start(bf16[48,4608]{1,0:T(8,128)(2,1)S(1)} %collective-permute-done.9.refs_8_) | copy-start | bytes 1327108
  48.3 22.5 %copy-start.17 = (bf16[48,4608]{1,0:T(8,128)(2,1)}, bf16[48,4608]{1,0:T(8,128)(2,1)S(1)}, u32[]{:S(2)}) copy-start(bf16[48,4608]{1,0:T(8,128)(2,1)S(1)} %collective-permute-done.8.refs_2_) | copy-start | bytes 1327108
  48.3 14.3 %collective-permute-start.13 = (bf16[48,2304]{1,0:T(8,128)(2,1)S(1)}, bf16[48,2304]{1,0:T(8,128)(2,1)S(1)}, u32[]{:S(2)}, u32[]{:S(2)}) collective-permute-start(bf16[48,2304]{1,0:T(8,128)(2,1)S(1)} %slice.72), channel_id=1, source_target_pairs={{0,8},{8,16},{16,24},{24,0},{1,9},{9,17},{17,25},{25,1},{2,10},{10... | collective-permute-start | bytes 663560 | tf_op jit(solution)/shard_map/ppermute | solution.py:36
  49.2 13.5 %collective-permute-start.12 = (bf16[48,2304]{1,0:T(8,128)(2,1)S(1)}, bf16[48,2304]{1,0:T(8,128)(2,1)S(1)}, u32[]{:S(2)}, u32[]{:S(2)}) collective-permute-start(bf16[48,2304]{1,0:T(8,128)(2,1)S(1)} %slice.71), channel_id=1, source_target_pairs={{0,24},{8,0},{16,8},{24,16},{1,25},{9,1},{17,9},{25,17},{2,26},{10... | collective-permute-start | bytes 663560 | tf_op jit(solution)/shard_map/ppermute | solution.py:36
  51.7 8.5 %collective-permute-start.10 = (bf16[16,4608]{1,0:T(8,128)(2,1)S(1)}, bf16[16,4608]{1,0:T(8,128)(2,1)S(1)}, u32[]{:S(2)}, u32[]{:S(2)}) collective-permute-start(bf16[16,4608]{1,0:T(8,128)(2,1)S(1)} %collective-permute-done.6.refs_0_), channel_id=1, source_target_pairs={{0,7},{1,0},{2,1},{3,2},{4,3},{5,4},{6,5},{7,6},{8,15},{9,8},{10,9... | collective-permute-start | bytes 442376 | tf_op jit(solution)/shard_map/ppermute | solution.py:36
  53.0 9.7 %collective-permute-start.11 = (bf16[16,4608]{1,0:T(8,128)(2,1)S(1)}, bf16[16,4608]{1,0:T(8,128)(2,1)S(1)}, u32[]{:S(2)}, u32[]{:S(2)}) collective-permute-start(bf16[16,4608]{1,0:T(8,128)(2,1)S(1)} %collective-permute-done.7.refs_4_), channel_id=1, source_target_pairs={{0,1},{1,2},{2,3},{3,4},{4,5},{5,6},{6,7},{7,0},{8,9},{9,10},{10,1... | collective-permute-start | bytes 442376 | tf_op jit(solution)/shard_map/ppermute | solution.py:36
  62.7 8.1 %copy-start.25 = (bf16[48,2304]{1,0:T(8,128)(2,1)}, bf16[48,2304]{1,0:T(8,128)(2,1)S(1)}, u32[]{:S(2)}) copy-start(bf16[48,2304]{1,0:T(8,128)(2,1)S(1)} %collective-permute-done.13.refs_5_) | copy-start | bytes 663556
  63.4 7.4 %collective-permute-start.15 = (bf16[16,2304]{1,0:T(8,128)(2,1)S(1)}, bf16[16,2304]{1,0:T(8,128)(2,1)S(1)}, u32[]{:S(2)}, u32[]{:S(2)}) collective-permute-start(bf16[16,2304]{1,0:T(8,128)(2,1)S(1)} %slice.74), channel_id=1, source_target_pairs={{0,1},{1,2},{2,3},{3,4},{4,5},{5,6},{6,7},{7,0},{8,9},{9,10},{10,1... | collective-permute-start | bytes 221192 | tf_op jit(solution)/shard_map/ppermute | solution.py:36
  63.7 7.1 %collective-permute-start.14 = (bf16[16,2304]{1,0:T(8,128)(2,1)S(1)}, bf16[16,2304]{1,0:T(8,128)(2,1)S(1)}, u32[]{:S(2)}, u32[]{:S(2)}) collective-permute-start(bf16[16,2304]{1,0:T(8,128)(2,1)S(1)} %slice.73), channel_id=1, source_target_pairs={{0,7},{1,0},{2,1},{3,2},{4,3},{5,4},{6,5},{7,6},{8,15},{9,8},{10,9... | collective-permute-start | bytes 221192 | tf_op jit(solution)/shard_map/ppermute | solution.py:36
  70.9 15.0 %collective-permute-start.17 = (bf16[80,4608]{1,0:T(8,128)(2,1)S(1)}, bf16[80,4608]{1,0:T(8,128)(2,1)S(1)}, u32[]{:S(2)}, u32[]{:S(2)}) collective-permute-start(bf16[80,4608]{1,0:T(8,128)(2,1)S(1)} %shard_map.108.refs_1_), channel_id=1, source_target_pairs={{0,8},{8,16},{16,24},{24,0},{1,9},{9,17},{17,25},{25,1},{2,10},{10... | collective-permute-start | bytes 2211848 | tf_op jit(solution)/shard_map/ppermute | solution.py:36
  71.0 14.9 %collective-permute-start.16 = (bf16[80,4608]{1,0:T(8,128)(2,1)S(1)}, bf16[80,4608]{1,0:T(8,128)(2,1)S(1)}, u32[]{:S(2)}, u32[]{:S(2)}) collective-permute-start(bf16[80,4608]{1,0:T(8,128)(2,1)S(1)} %shard_map.108.refs_1_), channel_id=1, source_target_pairs={{0,24},{8,0},{16,8},{24,16},{1,25},{9,1},{17,9},{25,17},{2,26},{10... | collective-permute-start | bytes 2211848 | tf_op jit(solution)/shard_map/ppermute | solution.py:36
  75.1 35.5 %collective-permute-start.19 = (bf16[768,1024]{1,0:T(8,128)(2,1)S(1)}, bf16[768,1024]{1,0:T(8,128)(2,1)}, u32[]{:S(2)}, u32[]{:S(2)}) collective-permute-start(bf16[768,1024]{1,0:T(8,128)(2,1)S(1)} %shard_map.104.refs_0_), channel_id=1, source_target_pairs={{0,64},{64,0},{1,65},{65,1},{2,66},{66,2},{3,67},{67,3},{4,68},{68... | collective-permute-start | bytes 4718600 | tf_op jit(solution)/shard_map/ppermute | solution.py:36
  85.9 1.7 copy-start.13
  85.9 24.7 %collective-permute-start.20 = (bf16[768,1024]{1,0:T(8,128)(2,1)S(1)}, bf16[768,1024]{1,0:T(8,128)(2,1)}, u32[]{:S(2)}, u32[]{:S(2)}) collective-permute-start(bf16[768,1024]{1,0:T(8,128)(2,1)S(1)} %collective-permute-done.18.refs_1_), channel_id=1, source_target_pairs={{0,64},{64,0},{1,65},{65,1},{2,66},{66,2},{3,67},{67,3},{4,68},{68... | collective-permute-start | bytes 4718600 | tf_op jit(solution)/shard_map/ppermute | solution.py:36
  87.6 12.3 %collective-permute-start.22 = (bf16[80,2304]{1,0:T(8,128)(2,1)}, bf16[80,2304]{1,0:T(8,128)(2,1)S(1)}, u32[]{:S(2)}, u32[]{:S(2)}) collective-permute-start(bf16[80,2304]{1,0:T(8,128)(2,1)} %slice.76), channel_id=1, source_target_pairs={{0,8},{8,16},{16,24},{24,0},{1,9},{9,17},{17,25},{25,1},{2,10},{10... | collective-permute-start | bytes 1105928 | tf_op jit(solution)/shard_map/ppermute | solution.py:36
  87.6 12.3 %collective-permute-start.21 = (bf16[80,2304]{1,0:T(8,128)(2,1)}, bf16[80,2304]{1,0:T(8,128)(2,1)}, u32[]{:S(2)}, u32[]{:S(2)}) collective-permute-start(bf16[80,2304]{1,0:T(8,128)(2,1)} %slice.75), channel_id=1, source_target_pairs={{0,24},{8,0},{16,8},{24,16},{1,25},{9,1},{17,9},{25,17},{2,26},{10... | collective-permute-start | bytes 1105928 | tf_op jit(solution)/shard_map/ppermute | solution.py:36
  99.9 1.1 copy-start.6
  102.0 1.1 copy-start.12
  103.2 1.1 copy-start.14
  114.8 2.2 copy-start
  117.8 2.3 %copy-start.3 = (bf16[576,4096]{1,0:T(8,128)(2,1)S(1)}, bf16[576,4096]{1,0:T(8,128)(2,1)}, u32[]{:S(2)}) copy-start(bf16[576,4096]{1,0:T(8,128)(2,1)} %all-gather.2.cloned.1.call-done.x_ref.right_ref) | copy-start | bytes 14155780
  120.2 5.7 %copy-start.8 = (f32[576,256]{1,0:T(8,128)S(1)}, f32[576,256]{1,0:T(8,128)}, u32[]{:S(2)}) copy-start(f32[576,256]{1,0:T(8,128)} %copy-done.7) | copy-start | bytes 1769476
  131.3 2.2 copy-start.2
  134.5 2.3 %copy-start.1 = (bf16[576,4096]{1,0:T(8,128)(2,1)S(1)}, bf16[576,4096]{1,0:T(8,128)(2,1)}, u32[]{:S(2)}) copy-start(bf16[576,4096]{1,0:T(8,128)(2,1)} %copy-done) | copy-start | bytes 14155780
  136.8 3.7 %copy-start.20 = (bf16[8,72,512]{2,1,0:T(8,128)(2,1)S(1)}, bf16[8,72,512]{2,1,0:T(8,128)(2,1)}, u32[]{:S(2)}) copy-start(bf16[8,72,512]{2,1,0:T(8,128)(2,1)} %copy-done.19) | copy-start | bytes 1769476
  140.4 7.9 %collective-permute-start.27 = (bf16[2,256,1024]{2,1,0:T(8,128)(2,1)S(1)}, bf16[2,256,1024]{2,1,0:T(8,128)(2,1)S(1)}, u32[]{:S(2)}, u32[]{:S(2)}) collective-permute-start(bf16[2,256,1024]{2,1,0:T(8,128)(2,1)S(1)} %get-tuple-element.70), channel_id=1, source_target_pairs={{0,64},{64,0},{1,65},{65,1},{2,66},{66,2},{3,67},{67,3},{4,68},{68... | collective-permute-start | bytes 3145736 | tf_op jit(solution)/shard_map/ppermute | solution.py:36
  140.5 2.3 %copy-start.4 = (bf16[576,4096]{1,0:T(8,128)(2,1)S(1)}, bf16[576,4096]{1,0:T(8,128)(2,1)}, u32[]{:S(2)}) copy-start(bf16[576,4096]{1,0:T(8,128)(2,1)} %all-gather.2.cloned.1.call-done.x_ref.right_ref) | copy-start | bytes 14155780
  148.4 4.4 %collective-permute-start.28 = (bf16[2,512,1024]{2,1,0:T(8,128)(2,1)S(1)}, bf16[2,512,1024]{2,1,0:T(8,128)(2,1)S(1)}, u32[]{:S(2)}, u32[]{:S(2)}) collective-permute-start(bf16[2,512,1024]{2,1,0:T(8,128)(2,1)S(1)} %get-tuple-element.73), channel_id=1, source_target_pairs={{0,64},{64,0},{1,65},{65,1},{2,66},{66,2},{3,67},{67,3},{4,68},{68... | collective-permute-start | bytes 6291464 | tf_op jit(solution)/shard_map/ppermute | solution.py:36
  153.8 2.6 %copy-start.33 = (f32[2,512,1024]{2,1,0:T(8,128)}, f32[2,512,1024]{2,1,0:T(8,128)S(1)}, u32[]{:S(2)}) copy-start(f32[2,512,1024]{2,1,0:T(8,128)S(1)} %convert_add_fusion) | copy-start | bytes 12582916
  155.1 40.5 %collective-permute-start.29 = (bf16[512,1024]{1,0:T(8,128)(2,1)}, bf16[512,1024]{1,0:T(8,128)(2,1)S(1)}, u32[]{:S(2)}, u32[]{:S(2)}) collective-permute-start(bf16[512,1024]{1,0:T(8,128)(2,1)} %fusion.1), channel_id=1, source_target_pairs={{0,128},{128,0},{1,129},{129,1},{2,130},{130,2},{3,131},{131,3},{4... | collective-permute-start | bytes 3145736 | tf_op jit(solution)/shard_map/ppermute | solution.py:36
  157.3 36.3 %collective-permute-start.30 = (bf16[256,1024]{1,0:T(8,128)(2,1)}, bf16[256,1024]{1,0:T(8,128)(2,1)}, u32[]{:S(2)}, u32[]{:S(2)}) collective-permute-start(bf16[256,1024]{1,0:T(8,128)(2,1)} %fusion.5), channel_id=1, source_target_pairs={{0,128},{128,0},{1,129},{129,1},{2,130},{130,2},{3,131},{131,3},{4... | collective-permute-start | bytes 1572872 | tf_op jit(solution)/shard_map/ppermute | solution.py:36
  198.6 8.0 %collective-permute-start.23 = (bf16[18,4096]{1,0:T(8,128)(2,1)S(1)}, bf16[18,4096]{1,0:T(8,128)(2,1)S(1)}, u32[]{:S(2)}, u32[]{:S(2)}) collective-permute-start(bf16[18,4096]{1,0:T(8,128)(2,1)S(1)} %get-tuple-element.65), channel_id=1, source_target_pairs={{0,8},{8,16},{16,24},{24,0},{1,9},{9,17},{17,25},{25,1},{2,10},{10... | collective-permute-start | bytes 442376 | tf_op jit(solution)/shard_map/ppermute | solution.py:36
  199.9 11.9 %collective-permute-start.24 = (bf16[18,4096]{1,0:T(8,128)(2,1)S(1)}, bf16[18,4096]{1,0:T(8,128)(2,1)S(1)}, u32[]{:S(2)}, u32[]{:S(2)}) collective-permute-start(bf16[18,4096]{1,0:T(8,128)(2,1)S(1)} %get-tuple-element.66), channel_id=1, source_target_pairs={{0,16},{8,24},{16,0},{24,8},{1,17},{9,25},{17,1},{25,9},{2,18},{10... | collective-permute-start | bytes 442376 | tf_op jit(solution)/shard_map/ppermute | solution.py:36
  203.2 8.6 %collective-permute-start.25 = (bf16[18,4096]{1,0:T(8,128)(2,1)S(1)}, bf16[18,4096]{1,0:T(8,128)(2,1)S(1)}, u32[]{:S(2)}, u32[]{:S(2)}) collective-permute-start(bf16[18,4096]{1,0:T(8,128)(2,1)S(1)} %get-tuple-element.67), channel_id=1, source_target_pairs={{0,24},{8,0},{16,8},{24,16},{1,25},{9,1},{17,9},{25,17},{2,26},{10... | collective-permute-start | bytes 442376 | tf_op jit(solution)/shard_map/ppermute | solution.py:36
  211.9 5.1 %collective-permute-start.26 = (bf16[9,4096]{1,0:T(8,128)(2,1)S(1)}, bf16[9,4096]{1,0:T(8,128)(2,1)S(1)}, u32[]{:S(2)}, u32[]{:S(2)}) collective-permute-start(bf16[9,4096]{1,0:T(8,128)(2,1)S(1)} %slice.165), channel_id=1, source_target_pairs={{0,32},{32,0},{1,33},{33,1},{2,34},{34,2},{3,35},{35,3},{4,36},{36... | collective-permute-start | bytes 221192 | tf_op jit(solution)/shard_map/ppermute | solution.py:36
  (19 other events, 17.5 us)
Sparse Core Ops, SparseCore 0:
  32.6 65.0 all-gather.1
  134.5 58.5 reduce-scatter.1
